TPU v7x, 32 devices: a whole 2x2x4 slice. The times are simulated.
32 devices in a mesh: group: 2 (over y), passage: 4 (over z), span: 4 (over x, core).
Axes of the slice: x: 2, y: 2, z: 4, core: 2. Of those that a mesh axis runs over, the one named last changes fastest.
Arguments:
- flow_state: float32 [64, 1024, 4096], P('group', 'span', 'passage'), parts along dimension 0, may hold values from -6 to 6
- swirl_speed: float32 [2048], P(('group', 'span')), parts along dimension 0, may hold values from -0.8 to 0.8
- diffusivity: float32 [2048, 4096], P(('group', 'span'), 'passage'), parts along dimension 0, may hold values from 0.02 to 0.2
- plane_index: int32 [16], P('group'), parts along dimension 0, may hold values from 0 to 31, as said below
- radial_modes: float32 [64, 1024], P(None, 'span'), may hold values from -0.1875 to 0.1875
- mode_order: int32 [64], replicated, may hold values from 0 to 63, each once
Outputs:
- next_state: float32 [64, 1024, 4096], P('group', 'span', 'passage'), parts along dimension 0
- amplitudes: float32 [16, 64, 256], P('group'), parts along dimension 0
There are 2 independent parts, one for each index of `group`. A program takes and returns all parts, laid end to end along the dimension named above; an argument that names none is the same for every part. Nothing has to cross between parts.
Inputs may be any that keep to these rules, and one draw needn't show every extreme that they name: `plane_index`: distinct stations, one of them station 32 - 1. `mode_order`: each number once.
All inputs are finite; a program needn't handle non-finite values.
Results may differ from a plain program's by a relative error of at most 0.000071.
Values sent between devices are 32-bit elements; how exact they have to be, the bound alone decides.
A program may use at most 128 MiB of HBM per device.

v0:
```python
import math

import jax
import jax.numpy as jnp
from jax import lax
from jax.sharding import PartitionSpec as P

NTH = 4096
BLADES = 16
K = 128


def with_halo(block, sides, width, periodic):
    for axis, dim in sides:
        count = lax.axis_size(axis)
        forward = [(i, i + 1) for i in range(count - 1)]
        if periodic:
            forward.append((count - 1, 0))
        backward = [(target, source) for source, target in forward]
        low = lax.ppermute(
            lax.slice_in_dim(block, block.shape[dim] - width, None, axis=dim), axis, forward
        )
        high = lax.ppermute(lax.slice_in_dim(block, 0, width, axis=dim), axis, backward)
        block = jnp.concatenate([low, block, high], axis=dim)
    return block


def spectra_basis(offset, extent, period, harmonics, blades):
    azimuth = (offset + jnp.arange(extent, dtype=jnp.int32))[:, None]
    harmonic = (jnp.arange(harmonics, dtype=jnp.int32) * blades)[None, :]
    phases = azimuth * harmonic % period
    angles = phases.astype(jnp.float32) * (2.0 * math.pi / period)
    return jnp.concatenate([jnp.cos(angles), -jnp.sin(angles)], axis=1) * (1.0 / math.sqrt(period))


def stencil(center, cycle_padded, radial_padded, swirl_speed, diffusivity):
    east_cell = cycle_padded[:, :, 2:]
    west_cell = cycle_padded[:, :, :-2]
    outer_cell = radial_padded[:, 2:, :]
    inner_cell = radial_padded[:, :-2, :]
    return (
        center
        - 0.5 * swirl_speed[None, :, None] * (east_cell - west_cell)
        + diffusivity[None] * (east_cell + west_cell + outer_cell + inner_cell - 4.0 * center)
    )


def body(flow_state, swirl_speed, diffusivity, plane_index, radial_modes, mode_order):
    cycle_padded = with_halo(flow_state, (("passage", 2),), 1, True)
    radial_padded = with_halo(flow_state, (("span", 1),), 1, False)
    cols_dev = flow_state.shape[2]
    position = lax.axis_index("passage")
    picked = jnp.take(radial_modes, mode_order, axis=0)
    next_state = stencil(flow_state, cycle_padded, radial_padded, swirl_speed, diffusivity)
    chosen = jnp.take(next_state, plane_index, axis=0)
    basis = spectra_basis(position * cols_dev, cols_dev, NTH, K, BLADES)
    spectra = jnp.einsum("prt,tc->prc", chosen, basis, precision=lax.Precision.HIGHEST)
    partial_value = jnp.einsum("mr,prc->pmc", picked, spectra, precision=lax.Precision.HIGHEST)
    amplitudes = lax.psum(partial_value, ("passage", "span"))
    return (next_state, amplitudes)


def solution(mesh):
    return jax.shard_map(
        body,
        mesh=mesh,
        in_specs=(
            P("group", "span", "passage"),
            P(("group", "span")),
            P(("group", "span"), "passage"),
            P("group"),
            P(None, "span"),
            P(),
        ),
        out_specs=(P("group", "span", "passage"), P("group", None, None)),
        check_vma=False,
    )
```

profile of v0, /device:TPU:0, one launch (start us, length us, event | category | flops | bytes accessed | tf_op | source)
XLA Modules:
  0.0 235.5 jit_solution(9681580888091691931)
XLA Ops:
  7.2 0.0 copy-start
  7.2 0.0 copy-start.2
  7.2 0.0 all-reduce.2.cloned.1.call-start
  7.2 8.1 %fusion.26 = (f32[32,256,1]{2,1,0:T(8,128)}, f32[32,256,1]{2,1,0:T(8,128)}) fusion(f32[32,256,1024]{2,1,0:T(8,128)} %param.6), kind=kLoop, calls=%fused_computation.48 | loop fusion | bytes 131072 | tf_op jit(solution)/shard_map/slice | solution.py:21
  15.4 2.8 %copy.17 = f32[32,256,1]{1,0,2:T(8,128)S(1)} copy(f32[32,256,1]{2,1,0:T(8,128)} %get-tuple-element.2) | data formatting | bytes 65536
  18.2 3.1 %collective-permute-start.1 = (f32[32,256,1]{1,0,2:T(8,128)S(1)}, f32[32,256,1]{1,0,2:T(8,128)S(1)}, u32[]{:S(2)}, u32[]{:S(2)}) collective-permute-start(f32[32,256,1]{1,0,2:T(8,128)S(1)} %copy.17), channel_id=1, source_target_pairs={{0,4},{4,8},{8,12},{12,0},{1,5},{5,9},{9,13},{13,1},{2,6},{6,10},{... | collective-permute-start | bytes 98312 | tf_op jit(solution)/shard_map/ppermute | solution.py:20
  21.2 2.8 %copy.16 = f32[32,256,1]{1,0,2:T(8,128)S(1)} copy(f32[32,256,1]{2,1,0:T(8,128)} %get-tuple-element.3) | data formatting | bytes 65536
  24.1 2.1 collective-permute-start
  26.2 1.8 fusion.27
  28.0 1.3 collective-permute-start.2
  29.3 3.0 %collective-permute-start.3 = (f32[32,1,1024]{2,0,1:T(8,128)S(1)}, f32[32,1,1024]{2,0,1:T(8,128)S(1)}, u32[]{:S(2)}, u32[]{:S(2)}) collective-permute-start(f32[32,1,1024]{2,0,1:T(8,128)S(1)} %copy.19), channel_id=1, source_target_pairs={{0,1},{1,2},{2,3},{4,5},{5,6},{6,7},{8,9},{9,10},{10,11},{12,13},{... | collective-permute-start | bytes 393224 | tf_op jit(solution)/shard_map/ppermute | solution.py:20
  32.4 0.7 compare_select_fusion.1
  33.0 0.7 compare_and_fusion.1
  33.7 0.7 compare_select_fusion
  34.3 0.7 compare_and_fusion
  35.0 0.7 broadcast_multiply_fusion
  35.7 2.1 fusion.17
  37.8 0.0 copy-done
  37.9 0.7 gather_fusion.1
  38.5 0.0 collective-permute-done.1
  38.5 2.8 %copy.11 = f32[32,256,1]{2,1,0:T(8,128)} copy(f32[32,256,1]{1,0,2:T(8,128)S(1)} %collective-permute-done.1) | data formatting | bytes 65536 | tf_op jit(solution)/shard_map/ppermute | solution.py:20
  41.4 0.0 collective-permute-done
  41.4 2.6 %copy.9 = f32[32,256,1]{2,1,0:T(8,128)} copy(f32[32,256,1]{1,0,2:T(8,128)S(1)} %collective-permute-done) | data formatting | bytes 65536 | tf_op jit(solution)/shard_map/ppermute | solution.py:23
  44.0 0.0 collective-permute-done.2
  44.0 0.1 copy.13
  44.1 0.0 collective-permute-done.3
  44.1 0.1 copy.15
  44.3 0.0 copy-done.2
  44.3 0.0 copy-start.1
  44.3 73.5 %fusion.3 = f32[32,256,1024]{2,1,0:T(8,128)} fusion(f32[32,256,1024]{2,1,0:T(8,128)} %param.6, f32[32,1,1024]{2,1,0:T(1,128)S(1)} %copy.15, f32[32,1,1024]{2,1,0:T(1,128)S(1)} %copy.13, f32[32,256,1]{2,1,0:T(8,128)} %copy.9, f32[32,256,1]{2,1,0:T(8,128)} %copy.11, f32[256,1024]{1,0:T(8,128)S(1)} %copy-done.2, f32[256]{0:T(256)S(1)} %broadcast_multiply_fusion), kind=kLoop, calls=%fused_computation.6 | loop fusion | flops 117440512 | bytes 68486144 | tf_op jit(solution)/shard_map/add | solution.py:42
  117.8 7.7 %gather_fusion = f32[8,256,1024]{2,1,0:T(8,128)} fusion(f32[32,256,1024]{2,1,0:T(8,128)} %fusion.3, s32[1024]{0:T(1024)S(1)} %pad_clamp_fusion.1), kind=kCustom, calls=%fused_computation | custom fusion | bytes 16777248 | tf_op jit(solution)/shard_map/jit(_take)/gather | solution.py:55
  125.5 9.1 %fusion.5 = f32[8,256,256]{2,1,0:T(8,128)S(1)} fusion(f32[8,256,1024]{2,1,0:T(8,128)} %gather_fusion, pred[8]{0:T(512)(128)(4,1)S(1)} %compare_and_fusion.1, f32[1024,128]{1,0:T(8,128)S(1)} %get-tuple-element.7, f32[1024,128]{1,0:T(8,128)S(1)} %get-tuple-element.6), kind=kOutput, calls=%fused_computation.11 | convolution fusion | flops 6445072384 | bytes 11534344 | tf_op jit(solution)/shard_map/prt,tc->prc/dot_general | solution.py:57
  134.6 2.3 convolution_bitcast_fusion
  136.9 0.0 all-reduce.2.cloned.1.call-update
  136.9 89.9 %all-reduce.2.cloned.1.call-done = f32[8,64,256]{2,1,0:T(8,128)} async-done(((f32[8,64,256]{2,1,0:T(8,128)}), f32[8,64,256]{2,1,0:T(8,128)}) %all-reduce.2.cloned.1.call-update) | async-done | bytes 524304 | tf_op jit(solution)/shard_map/psum | solution.py:59
  226.8 1.9 copy.21
  228.7 0.0 copy-done.1
  (6 shorter events, 0.1 us)
Async XLA Ops:
  7.2 30.7 %copy-start = (f32[64,256]{1,0:T(8,128)S(1)}, f32[64,256]{1,0:T(8,128)}, u32[]{:S(2)}) copy-start(f32[64,256]{1,0:T(8,128)} %param.10) | copy-start | bytes 196612
  7.2 37.1 %copy-start.2 = (f32[256,1024]{1,0:T(8,128)S(1)}, f32[256,1024]{1,0:T(8,128)}, u32[]{:S(2)}) copy-start(f32[256,1024]{1,0:T(8,128)} %param.8) | copy-start | bytes 3145732
  7.2 219.6 %all-reduce.2.cloned.1.call-start = ((), (), s32[]{:S(2)}) async-start(), calls=%async_computation | async-start | bytes 1048576 | tf_op jit(solution)/shard_map/psum | solution.py:59
  18.2 20.3 %collective-permute-start.1 = (f32[32,256,1]{1,0,2:T(8,128)S(1)}, f32[32,256,1]{1,0,2:T(8,128)S(1)}, u32[]{:S(2)}, u32[]{:S(2)}) collective-permute-start(f32[32,256,1]{1,0,2:T(8,128)S(1)} %copy.17), channel_id=1, source_target_pairs={{0,4},{4,8},{8,12},{12,0},{1,5},{5,9},{9,13},{13,1},{2,6},{6,10},{... | collective-permute-start | bytes 98312 | tf_op jit(solution)/shard_map/ppermute | solution.py:20
  24.1 17.3 %collective-permute-start = (f32[32,256,1]{1,0,2:T(8,128)S(1)}, f32[32,256,1]{1,0,2:T(8,128)S(1)}, u32[]{:S(2)}, u32[]{:S(2)}) collective-permute-start(f32[32,256,1]{1,0,2:T(8,128)S(1)} %copy.16), channel_id=1, source_target_pairs={{4,0},{8,4},{12,8},{0,12},{5,1},{9,5},{13,9},{1,13},{6,2},{10,6},{... | collective-permute-start | bytes 98312 | tf_op jit(solution)/shard_map/ppermute | solution.py:23
  28.0 16.0 %collective-permute-start.2 = (f32[32,1,1024]{2,0,1:T(8,128)S(1)}, f32[32,1,1024]{2,0,1:T(8,128)S(1)}, u32[]{:S(2)}, u32[]{:S(2)}) collective-permute-start(f32[32,1,1024]{2,0,1:T(8,128)S(1)} %copy.18), channel_id=1, source_target_pairs={{1,0},{2,1},{3,2},{5,4},{6,5},{7,6},{9,8},{10,9},{11,10},{13,12},{... | collective-permute-start | bytes 393224 | tf_op jit(solution)/shard_map/ppermute | solution.py:23
  29.3 14.8 %collective-permute-start.3 = (f32[32,1,1024]{2,0,1:T(8,128)S(1)}, f32[32,1,1024]{2,0,1:T(8,128)S(1)}, u32[]{:S(2)}, u32[]{:S(2)}) collective-permute-start(f32[32,1,1024]{2,0,1:T(8,128)S(1)} %copy.19), channel_id=1, source_target_pairs={{0,1},{1,2},{2,3},{4,5},{5,6},{6,7},{8,9},{9,10},{10,11},{12,13},{... | collective-permute-start | bytes 393224 | tf_op jit(solution)/shard_map/ppermute | solution.py:20
  44.3 184.4 %copy-start.1 = (f32[64,256]{1,0:T(8,128)S(1)}, f32[64,256]{1,0:T(8,128)}, u32[]{:S(2)}) copy-start(f32[64,256]{1,0:T(8,128)} %param.10) | copy-start | bytes 196612
Sparse Core Ops, SparseCore 0:
  137.1 89.7 all-reduce.1
where the time goes:
time: 236 us
  waiting for transfers between devices  89.9 us (38%)
  other arithmetic  78.9 us (33%)
  local copies, waits for them, and re-layouts  31.6 us (13%)
  between operations  14.2 us (6%)
  matrix products  11.4 us (5%)
  starting transfers between devices  9.52 us (4%)
    psum x1, waiting for transfers between devices, body(): amplitudes = lax.psum(partial_value, ('passage', 'span'))  89.9 us
    add x1, other arithmetic, stencil(): center - 0.5 * swirl_speed[None, :, None] * (east_cell - west_cell)  73.5 us
    dot_general x1, matrix products, body(): jnp.einsum('prt,tc->prc', chosen, basis, precision=lax.Precision.HIGHEST)  9.13 us
    slice x1, local copies, waits for them, and re-layouts, with_halo(): lax.slice_in_dim(block, block.shape[dim] - width, None, axis=dim)  8.11 us
    gather x1, local copies, waits for them, and re-layouts, body(): chosen = jnp.take(next_state, plane_index, axis=0)  7.71 us
    unnamed x11, local copies, waits for them, and re-layouts  7.6 us
    ppermute x2, starting transfers between devices, with_halo(): lax.ppermute(lax.slice_in_dim(block, block.shape[dim] - width, None, axis...  6.1 us
  transfers between devices with their start and end apart: 5, of which 1 were waited for; matrix products, arithmetic and copies ran while one was open for 7% of the time, Pallas kernels for 0%

commit v1 on v0

v1 whole, which is shorter than its diff:
```python
import functools
import math

import jax
import jax.numpy as jnp
import numpy as np
from jax import lax
from jax.experimental import pallas as pl
from jax.experimental.pallas import tpu as pltpu
from jax.sharding import PartitionSpec as P

NTH = 4096
BLADES = 16
K = 128
PERIOD = NTH // BLADES
LANES = 128
MIB = 1024 * 1024
MESH = pl.DeviceIdType.MESH


def dft_basis():
    t = np.arange(PERIOD)[:, None]
    k = np.arange(K)[None, :]
    angles = (t * k % PERIOD) * (2.0 * math.pi / PERIOD)
    both = np.concatenate([np.cos(angles), -np.sin(angles)], axis=1)
    return (both / math.sqrt(NTH)).astype(np.float32)


def halo_kernel(
    passages, spans, chunks, flow, rows_out, cols_out,
    left, right, low, high, rows_send, cols_send, load_sem, send_sem, recv_sem,
):
    stations, rows, cols = flow.shape
    passage = lax.axis_index("passage")
    span = lax.axis_index("span")
    groups = LANES // stations
    per = rows // groups
    step = stations // chunks

    def loads(c):
        part = pl.ds(c * step, step)
        return [
            pltpu.make_async_copy(
                flow.at[part, :, pl.ds(0, LANES)], left.at[part], load_sem.at[2 + 2 * c]),
            pltpu.make_async_copy(
                flow.at[part, :, pl.ds(cols - LANES, LANES)], right.at[part],
                load_sem.at[3 + 2 * c]),
        ]

    row_loads = [
        pltpu.make_async_copy(flow.at[:, pl.ds(0, 8), :], low, load_sem.at[0]),
        pltpu.make_async_copy(flow.at[:, pl.ds(rows - 8, 8), :], high, load_sem.at[1]),
    ]
    for copy in row_loads:
        copy.start()
    for c in range(chunks):
        for copy in loads(c):
            copy.start()

    west = lax.rem(passage + passages - 1, passages)
    east = lax.rem(passage + 1, passages)
    outer = jnp.minimum(span + 1, spans - 1)
    inner = jnp.maximum(span - 1, 0)
    barrier = pltpu.get_barrier_semaphore()
    for side in (west, east):
        pl.semaphore_signal(barrier, inc=1, device_id={"passage": side}, device_id_type=MESH)
    for side in (1, spans - 1):
        pl.semaphore_signal(
            barrier, inc=1, device_id={"span": lax.rem(span + side, spans)}, device_id_type=MESH)
    pl.semaphore_wait(barrier, 4)

    to_inner = pltpu.make_async_remote_copy(
        src_ref=rows_send.at[0], dst_ref=rows_out.at[1], send_sem=send_sem.at[0],
        recv_sem=recv_sem.at[0], device_id={"span": inner}, device_id_type=MESH)
    to_outer = pltpu.make_async_remote_copy(
        src_ref=rows_send.at[1], dst_ref=rows_out.at[0], send_sem=send_sem.at[1],
        recv_sem=recv_sem.at[1], device_id={"span": outer}, device_id_type=MESH)
    to_west = pltpu.make_async_remote_copy(
        src_ref=cols_send.at[0], dst_ref=cols_out.at[1], send_sem=send_sem.at[2],
        recv_sem=recv_sem.at[2], device_id={"passage": west}, device_id_type=MESH)
    to_east = pltpu.make_async_remote_copy(
        src_ref=cols_send.at[1], dst_ref=cols_out.at[0], send_sem=send_sem.at[3],
        recv_sem=recv_sem.at[3], device_id={"passage": east}, device_id_type=MESH)

    for copy in row_loads:
        copy.wait()
    rows_send[0] = low[:, 0, :]
    rows_send[1] = high[:, 7, :]

    @pl.when(span > 0)
    def _():
        to_inner.start()

    @pl.when(span < spans - 1)
    def _():
        to_outer.start()

    @pl.when(span == 0)
    def _():
        rows_out[0] = jnp.zeros((stations, cols), jnp.float32)

    @pl.when(span == spans - 1)
    def _():
        rows_out[1] = jnp.zeros((stations, cols), jnp.float32)

    lane = lax.broadcasted_iota(jnp.int32, (per, LANES), 1)

    def pack(z, carry):
        a, b = carry
        for g in range(groups):
            spot = g * stations + z
            part = pl.ds(g * per, per)
            a = jnp.where(lane == spot, pltpu.roll(left[z, part, :], spot, 1), a)
            b = jnp.where(lane == spot, pltpu.roll(right[z, part, :], spot + 1, 1), b)
        return a, b

    zero = jnp.zeros((per, LANES), jnp.float32)
    carry = (zero, zero)
    for c in range(chunks):
        for copy in loads(c):
            copy.wait()
        carry = lax.fori_loop(c * step, (c + 1) * step, pack, carry)
    cols_send[0], cols_send[1] = carry
    to_west.start()
    to_east.start()
    to_west.wait()
    to_east.wait()

    @pl.when(span > 0)
    def _():
        to_inner.wait_send()
        to_outer.wait_recv()

    @pl.when(span < spans - 1)
    def _():
        to_outer.wait_send()
        to_inner.wait_recv()


def halo(flow, passages, spans):
    stations, rows, cols = flow.shape
    groups = LANES // stations
    chunks = 4
    f32 = jnp.float32
    vmem = pl.BlockSpec(memory_space=pltpu.VMEM)
    return pl.pallas_call(
        functools.partial(halo_kernel, passages, spans, chunks),
        out_shape=(
            jax.ShapeDtypeStruct((2, stations, cols), f32),
            jax.ShapeDtypeStruct((2, rows // groups, LANES), f32),
        ),
        in_specs=[pl.BlockSpec(memory_space=pl.ANY)],
        out_specs=(vmem, vmem),
        scratch_shapes=[
            pltpu.VMEM((stations, rows, LANES), f32),
            pltpu.VMEM((stations, rows, LANES), f32),
            pltpu.VMEM((stations, 8, cols), f32),
            pltpu.VMEM((stations, 8, cols), f32),
            pltpu.VMEM((2, stations, cols), f32),
            pltpu.VMEM((2, rows // groups, LANES), f32),
            pltpu.SemaphoreType.DMA((2 + 2 * chunks,)),
            pltpu.SemaphoreType.DMA((4,)),
            pltpu.SemaphoreType.DMA((4,)),
        ],
        compiler_params=pltpu.CompilerParams(
            collective_id=0, has_side_effects=True, vmem_limit_bytes=24 * MIB),
        name="halo",
    )(flow)


def stencil_kernel(
    planes, plane_index, mode_order, flow, rows_in, cols_in, swirl, diff, modes, basis,
    out, amp, coef_e, coef_w, coef_c, picked, fold,
):
    _, rows, cols = flow.shape
    stations = rows_in.shape[1]
    per = cols_in.shape[1]
    z = pl.program_id(0)

    @pl.when(z == 0)
    def _():
        d = diff[...]
        half = 0.5 * jnp.broadcast_to(swirl[...], (LANES, rows)).T
        half = jnp.concatenate([half] * (cols // LANES), axis=1)
        coef_e[...] = d - half
        coef_w[...] = d + half
        coef_c[...] = 1.0 - 4.0 * d
        for j in range(modes.shape[0]):
            picked[pl.ds(j, 1), :] = modes[pl.ds(mode_order[j], 1), :]

    lane = lax.broadcasted_iota(jnp.int32, (8, LANES), 1)
    sub = lax.broadcasted_iota(jnp.int32, (8, cols), 0)
    last = cols - LANES
    for r in range(0, rows, 8):
        part = slice(r, r + 8)
        center = flow[0, part, :]
        if r == 0:
            inner = jnp.where(sub == 0, rows_in[0, pl.ds(z, 1), :], pltpu.roll(center, 1, 0))
        else:
            inner = flow[0, r - 1:r + 7, :]
        if r == rows - 8:
            outer = jnp.where(sub == 7, rows_in[1, pl.ds(z, 1), :], pltpu.roll(center, 7, 0))
        else:
            outer = flow[0, r + 1:r + 9, :]
        spot = (r // per) * stations + z
        packed = slice(r % per, r % per + 8)
        west_edge = pltpu.roll(cols_in[0, packed, :], LANES - spot, 1)
        east_edge = pltpu.roll(cols_in[1, packed, :], LANES - 1 - spot, 1)
        east = pltpu.roll(center, cols - 1, 1)
        west = pltpu.roll(center, 1, 1)
        east = jnp.concatenate(
            [east[:, :last], jnp.where(lane == LANES - 1, east_edge, east[:, last:])], axis=1)
        west = jnp.concatenate(
            [jnp.where(lane == 0, west_edge, west[:, :LANES]), west[:, LANES:]], axis=1)
        value = (
            coef_c[part, :] * center + coef_e[part, :] * east + coef_w[part, :] * west
            + diff[part, :] * (outer + inner)
        )
        out[0, part, :] = value
        total = value[:, :PERIOD]
        for m in range(PERIOD, cols, PERIOD):
            total = total + value[:, m:m + PERIOD]
        fold[part, :] = total

    for p in range(planes):
        @pl.when(plane_index[p] == z)
        def _():
            shape = jnp.dot(
                picked[...], fold[...], precision=lax.Precision.HIGHEST,
                preferred_element_type=jnp.float32)
            lines = jnp.dot(
                shape, basis[...], precision=lax.Precision.HIGHEST,
                preferred_element_type=jnp.float32)
            tiles = lines.shape[0] // 8
            for h in range(2):
                amp[pl.ds((2 * p + h) * tiles, tiles)] = (
                    lines[:, h * LANES:(h + 1) * LANES].reshape(tiles, 8, LANES))


def stencil(flow, rows_in, cols_in, swirl, diff, plane_index, modes, mode_order):
    stations, rows, cols = flow.shape
    planes = plane_index.shape[0]
    m = modes.shape[0]
    f32 = jnp.float32
    smem = pl.BlockSpec(memory_space=pltpu.SMEM)
    plane = pl.BlockSpec((1, rows, cols), lambda z: (z, 0, 0))

    def whole(shape):
        return pl.BlockSpec(shape, lambda z: (0,) * len(shape))

    tiles = planes * m * 2 * K // (8 * LANES)
    return pl.pallas_call(
        functools.partial(stencil_kernel, planes),
        out_shape=(
            jax.ShapeDtypeStruct(flow.shape, f32),
            jax.ShapeDtypeStruct((tiles, 8, LANES), f32),
        ),
        grid=(stations,),
        in_specs=[
            smem, smem, plane, whole(rows_in.shape), whole(cols_in.shape), whole((1, rows)),
            whole(diff.shape), whole(modes.shape), whole((PERIOD, 2 * K)),
        ],
        out_specs=(plane, whole((tiles, 8, LANES))),
        scratch_shapes=[
            pltpu.VMEM((rows, cols), f32),
            pltpu.VMEM((rows, cols), f32),
            pltpu.VMEM((rows, cols), f32),
            pltpu.VMEM((m, rows), f32),
            pltpu.VMEM((rows, PERIOD), f32),
        ],
        compiler_params=pltpu.CompilerParams(vmem_limit_bytes=32 * MIB),
        name="stencil",
    )(plane_index, mode_order, flow, rows_in, cols_in, swirl.reshape(1, rows), diff, modes,
      jnp.asarray(dft_basis()))


def sum_kernel(sizes, amp, out, acc, full, *rest):
    recvs, (send_sem, recv_sem, send_sem2, recv_sem2) = rest[:3], rest[3:]
    cores, xs, zs = sizes
    span = lax.axis_index("span")
    core, x, z = lax.rem(span, cores), span // cores, lax.axis_index("passage")
    mine = (core, x, z)

    def peer(s, k):
        if s == 0:
            return {"span": x * cores + k}
        if s == 1:
            return {"span": k * cores + core}
        return {"passage": k}

    def others(s):
        return [(d, lax.rem(mine[s] + d, sizes[s])) for d in range(1, sizes[s])]

    barrier = pltpu.get_barrier_semaphore()
    for s in range(3):
        for _, k in others(s):
            pl.semaphore_signal(barrier, inc=1, device_id=peer(s, k), device_id_type=MESH)
    pl.semaphore_wait(barrier, sum(sizes) - 3)

    size = amp.shape[0]
    base = 0
    bases, widths = [], []
    index = 0
    firsts = []
    for s in range(3):
        width = size // sizes[s]
        source = amp if s == 0 else acc
        firsts.append(index)
        copies = []
        for d, k in others(s):
            copy = pltpu.make_async_remote_copy(
                src_ref=source.at[pl.ds(base + k * width, width)], dst_ref=recvs[s].at[d - 1],
                send_sem=send_sem.at[index], recv_sem=recv_sem.at[index],
                device_id=peer(s, k), device_id_type=MESH)
            copy.start()
            copies.append(copy)
            index += 1
        base = base + mine[s] * width
        size = width
        bases.append(base)
        widths.append(width)
        for copy in copies:
            copy.wait()
        part = pl.ds(base, width)
        total = source[part]
        for d in range(1, sizes[s]):
            total = total + recvs[s][d - 1]
        if s < 2:
            acc[part] = total
        else:
            full[part] = total

    for s in (2, 1, 0):
        part = pl.ds(bases[s], widths[s])
        copies = []
        for d, k in others(s):
            at = firsts[s] + d - 1
            copy = pltpu.make_async_remote_copy(
                src_ref=full.at[part], dst_ref=full.at[part],
                send_sem=send_sem2.at[at], recv_sem=recv_sem2.at[at],
                device_id=peer(s, k), device_id_type=MESH)
            copy.start()
            copies.append(copy)
        for copy in copies:
            copy.wait()

    planes, m, _ = out.shape
    tiles = m // 8
    for p in range(planes):
        for h in range(2):
            out[p, :, h * LANES:(h + 1) * LANES] = (
                full[pl.ds((2 * p + h) * tiles, tiles)].reshape(m, LANES))


def amplitude_sum(amp, planes, m, sizes):
    f32 = jnp.float32
    tiles = amp.shape[0]
    widths = [tiles // math.prod(sizes[:s + 1]) for s in range(3)]
    total = sum(sizes) - 3
    vmem = pl.BlockSpec(memory_space=pltpu.VMEM)
    return pl.pallas_call(
        functools.partial(sum_kernel, sizes),
        out_shape=jax.ShapeDtypeStruct((planes, m, 2 * K), f32),
        in_specs=[vmem],
        out_specs=vmem,
        scratch_shapes=[
            pltpu.VMEM((tiles, 8, LANES), f32),
            pltpu.VMEM((tiles, 8, LANES), f32),
            *[pltpu.VMEM((max(n - 1, 1), w, 8, LANES), f32) for n, w in zip(sizes, widths)],
            *[pltpu.SemaphoreType.DMA((total,)) for _ in range(4)],
        ],
        compiler_params=pltpu.CompilerParams(
            collective_id=1, has_side_effects=True, vmem_limit_bytes=16 * MIB),
        name="amplitude_sum",
    )(amp)


def body(passages, spans, flow_state, swirl_speed, diffusivity, plane_index, radial_modes, mode_order):
    rows_in, cols_in = halo(flow_state, passages, spans)
    next_state, partial_value = stencil(
        flow_state, rows_in, cols_in, swirl_speed, diffusivity, plane_index, radial_modes, mode_order)
    sizes = (2, spans // 2, passages)
    amplitudes = amplitude_sum(partial_value, plane_index.shape[0], mode_order.shape[0], sizes)
    return (next_state, amplitudes)


def solution(mesh):
    return jax.shard_map(
        functools.partial(body, mesh.shape["passage"], mesh.shape["span"]),
        mesh=mesh,
        in_specs=(
            P("group", "span", "passage"),
            P(("group", "span")),
            P(("group", "span"), "passage"),
            P("group"),
            P(None, "span"),
            P(),
        ),
        out_specs=(P("group", "span", "passage"), P("group", None, None)),
        check_vma=False,
    )
```

time: 236 us -> 83.1 us (0.35)
  waiting for transfers between devices: 89.9 us -> 0 us
  Pallas kernels: 0 us -> 80.5 us
  other arithmetic: 78.9 us -> 0 us
  local copies, waits for them, and re-layouts: 31.6 us -> 0.82 us
  between operations: 14.2 us -> 0.74 us
  matrix products: 11.4 us -> 0 us
  starting transfers between devices: 9.52 us -> 0 us
    psum x1 -> x0, waiting for transfers between devices: 89.9 us -> none  [body(): amplitudes = lax.psum(partial_value, ('passage', 'span'))]
    pallas_call x0 -> x3, Pallas kernels: none -> 80.5 us  [the longest x1 44.9 us: stencil(): pl.pallas_call(functools.partial(stencil_kernel, planes), out_shape=(jax....]
    add x2 -> x0, other arithmetic: 73.5 us -> none  [the longest x1 73.5 us: stencil(): center - 0.5 * swirl_speed[None, :, None] * (east_cell - west_cell)]
    dot_general x2 -> x0, matrix products: 11.4 us -> none  [the longest x1 9.13 us: body(): jnp.einsum('prt,tc->prc', chosen, basis, precision=lax.Precision.HIGHEST)]
    slice x2 -> x0, local copies, waits for them, and re-layouts: 9.88 us -> none  [the longest x1 8.11 us: with_halo(): lax.slice_in_dim(block, block.shape[dim] - width, None, axis=dim)]
    ppermute x4 -> x0, starting transfers between devices: 9.48 us -> none  [the longest x2 6.1 us: with_halo(): lax.ppermute(lax.slice_in_dim(block, block.shape[dim] - width, None, axis...]
    gather x2 -> x0, local copies, waits for them, and re-layouts: 8.36 us -> none  [the longest x1 7.71 us: body(): chosen = jnp.take(next_state, plane_index, axis=0)]
    unnamed x11 -> x13, local copies, waits for them, and re-layouts: 7.6 us -> 0.82 us
  transfers between devices with their start and end apart: 5 -> 0, of which waited for: 1 -> 0; matrix products, arithmetic and copies ran while one was open for 7% -> 0% of each run, Pallas kernels for 0% -> 0%
where the time goes in v1:
time: 83.1 us; the launch traced here: 82.1 us
  Pallas kernels  80.5 us (97%)
    pallas_call x1, Pallas kernels, stencil(): pl.pallas_call(functools.partial(stencil_kernel, planes), out_shape=(jax....  44.9 us
    pallas_call x1, Pallas kernels, amplitude_sum(): pl.pallas_call(functools.partial(sum_kernel, sizes), out_shape=jax.ShapeD...  21.6 us
    pallas_call x1, Pallas kernels, halo(): pl.pallas_call(functools.partial(halo_kernel, passages, spans, chunks), o...  14 us

profile of v1, /device:TPU:0, one launch (start us, length us, event | category | flops | bytes accessed | tf_op | source)
XLA Modules:
  0.0 82.1 jit_solution(13511702451255048562)
XLA Ops:
  0.6 0.0 copy-start.1
  0.6 0.0 copy-start.5
  0.7 0.0 copy-start.2
  0.7 0.0 copy-start.4
  0.7 0.0 copy-start
  0.7 0.0 copy-start.3
  0.7 14.0 %halo.1 = (f32[2,32,1024]{2,1,0:T(8,128)S(1)}, f32[2,64,128]{2,1,0:T(8,128)S(1)}) custom-call(f32[32,256,1024]{2,1,0:T(8,128)} %flow.3), custom_call_target="tpu_custom_call" | custom-call | tf_op jit(solution)/shard_map/halo/pallas_call | solution.py:146
  14.8 0.0 copy-done.1
  14.8 0.0 copy-done.5
  14.8 0.0 copy-done.2
  14.8 0.0 copy-done.4
  14.8 0.0 copy-done
  14.8 0.0 copy-done.3
  14.8 44.9 %stencil.1 = (f32[32,256,1024]{2,1,0:T(8,128)}, f32[128,8,128]{2,1,0:T(8,128)S(1)}) custom-call(s32[8]{0:T(128)S(1)} %copy-done.4, s32[64]{0:T(128)S(1)} %copy-done.5, f32[32,256,1024]{2,1,0:T(8,128)} %flow.3, f32[2,32,1024]{2,1,0:T(8,128)S(1)} %get-tuple-element.6.rows_in, f32[2,64,128]{2,1,0:T(8,128)S(1)} %get-tuple-element.7.cols_in, ...), custom_call_target="tpu_custom_call" | custom-call | tf_op jit(solution)/shard_map/stencil/pallas_call | solution.py:252
  59.7 21.6 %amplitude_sum.1 = f32[8,64,256]{2,1,0:T(8,128)S(1)} custom-call(f32[128,8,128]{2,1,0:T(8,128)S(1)} %get-tuple-element.9.amp), custom_call_target="tpu_custom_call" | custom-call | tf_op jit(solution)/shard_map/amplitude_sum/pallas_call | solution.py:361
  81.3 0.8 copy.10
Async XLA Ops:
  0.6 14.1 %copy-start.1 = (f32[256,256]{1,0:T(8,128)S(1)}, f32[256,256]{1,0:T(8,128)}, u32[]{:S(2)}) copy-start(f32[256,256]{1,0:T(8,128)} %constant.2.clone.basis) | copy-start | bytes 786436
  0.6 14.1 %copy-start.5 = (s32[64]{0:T(128)S(1)}, s32[64]{0:T(128)}, u32[]{:S(2)}) copy-start(s32[64]{0:T(128)} %mode_order.1) | copy-start | bytes 772
  0.7 14.1 %copy-start.2 = (f32[64,256]{1,0:T(8,128)S(1)}, f32[64,256]{1,0:T(8,128)}, u32[]{:S(2)}) copy-start(f32[64,256]{1,0:T(8,128)} %modes.1) | copy-start | bytes 196612
  0.7 14.1 %copy-start.4 = (s32[8]{0:T(128)S(1)}, s32[8]{0:T(128)}, u32[]{:S(2)}) copy-start(s32[8]{0:T(128)} %plane_index.1) | copy-start | bytes 100
  0.7 14.1 %copy-start = (f32[256,1024]{1,0:T(8,128)S(1)}, f32[256,1024]{1,0:T(8,128)}, u32[]{:S(2)}) copy-start(f32[256,1024]{1,0:T(8,128)} %diff.1) | copy-start | bytes 3145732
  0.7 14.1 %copy-start.3 = (f32[256]{0:T(256)S(1)}, f32[256]{0:T(256)}, u32[]{:S(2)}) copy-start(f32[256]{0:T(256)} %param.8) | copy-start | bytes 3076

commit v2 on v1

--- a/solution.py
+++ b/solution.py
@@ -170,14 +170,15 @@
 
 def stencil_kernel(
     planes, plane_index, mode_order, flow, rows_in, cols_in, swirl, diff, modes, basis,
-    out, amp, coef_e, coef_w, coef_c, picked, fold,
+    out, amp, coef_e, coef_w, coef_c, picked, fold, shapes,
 ):
-    _, rows, cols = flow.shape
+    block, rows, cols = flow.shape
     stations = rows_in.shape[1]
     per = cols_in.shape[1]
-    z = pl.program_id(0)
-
-    @pl.when(z == 0)
+    m = modes.shape[0]
+    first = pl.program_id(0) * block
+
+    @pl.when(first == 0)
     def _():
         d = diff[...]
         half = 0.5 * jnp.broadcast_to(swirl[...], (LANES, rows)).T
@@ -185,7 +186,7 @@
         coef_e[...] = d - half
         coef_w[...] = d + half
         coef_c[...] = 1.0 - 4.0 * d
-        for j in range(modes.shape[0]):
+        for j in range(m):
             picked[pl.ds(j, 1), :] = modes[pl.ds(mode_order[j], 1), :]
 
     lane = lax.broadcasted_iota(jnp.int32, (8, LANES), 1)
@@ -193,57 +194,65 @@
     last = cols - LANES
     for r in range(0, rows, 8):
         part = slice(r, r + 8)
-        center = flow[0, part, :]
-        if r == 0:
-            inner = jnp.where(sub == 0, rows_in[0, pl.ds(z, 1), :], pltpu.roll(center, 1, 0))
-        else:
-            inner = flow[0, r - 1:r + 7, :]
-        if r == rows - 8:
-            outer = jnp.where(sub == 7, rows_in[1, pl.ds(z, 1), :], pltpu.roll(center, 7, 0))
-        else:
-            outer = flow[0, r + 1:r + 9, :]
-        spot = (r // per) * stations + z
-        packed = slice(r % per, r % per + 8)
-        west_edge = pltpu.roll(cols_in[0, packed, :], LANES - spot, 1)
-        east_edge = pltpu.roll(cols_in[1, packed, :], LANES - 1 - spot, 1)
-        east = pltpu.roll(center, cols - 1, 1)
-        west = pltpu.roll(center, 1, 1)
-        east = jnp.concatenate(
-            [east[:, :last], jnp.where(lane == LANES - 1, east_edge, east[:, last:])], axis=1)
-        west = jnp.concatenate(
-            [jnp.where(lane == 0, west_edge, west[:, :LANES]), west[:, LANES:]], axis=1)
-        value = (
-            coef_c[part, :] * center + coef_e[part, :] * east + coef_w[part, :] * west
-            + diff[part, :] * (outer + inner)
-        )
-        out[0, part, :] = value
-        total = value[:, :PERIOD]
-        for m in range(PERIOD, cols, PERIOD):
-            total = total + value[:, m:m + PERIOD]
-        fold[part, :] = total
+        of_e, of_w, of_c, of_d = coef_e[part, :], coef_w[part, :], coef_c[part, :], diff[part, :]
+        for b in range(block):
+            z = first + b
+            center = flow[b, part, :]
+            if r == 0:
+                inner = jnp.where(sub == 0, rows_in[0, pl.ds(z, 1), :], pltpu.roll(center, 1, 0))
+            else:
+                inner = flow[b, r - 1:r + 7, :]
+            if r == rows - 8:
+                outer = jnp.where(sub == 7, rows_in[1, pl.ds(z, 1), :], pltpu.roll(center, 7, 0))
+            else:
+                outer = flow[b, r + 1:r + 9, :]
+            spot = (r // per) * stations + z
+            packed = slice(r % per, r % per + 8)
+            west_edge = pltpu.roll(cols_in[0, packed, :], LANES - spot, 1)
+            east_edge = pltpu.roll(cols_in[1, packed, :], LANES - 1 - spot, 1)
+            east = pltpu.roll(center, cols - 1, 1)
+            west = pltpu.roll(center, 1, 1)
+            east = jnp.concatenate(
+                [east[:, :last], jnp.where(lane == LANES - 1, east_edge, east[:, last:])], axis=1)
+            west = jnp.concatenate(
+                [jnp.where(lane == 0, west_edge, west[:, :LANES]), west[:, LANES:]], axis=1)
+            value = of_c * center + of_e * east + of_w * west + of_d * (outer + inner)
+            out[b, part, :] = value
+            total = value[:, :PERIOD]
+            for c in range(PERIOD, cols, PERIOD):
+                total = total + value[:, c:c + PERIOD]
+            fold[b, part, :] = total
 
     for p in range(planes):
-        @pl.when(plane_index[p] == z)
+        b = plane_index[p] - first
+
+        @pl.when((b >= 0) & (b < block))
         def _():
-            shape = jnp.dot(
-                picked[...], fold[...], precision=lax.Precision.HIGHEST,
+            shapes[p * m:(p + 1) * m, :] = jnp.dot(
+                picked[...], fold[b], precision=lax.Precision.HIGHEST,
                 preferred_element_type=jnp.float32)
-            lines = jnp.dot(
-                shape, basis[...], precision=lax.Precision.HIGHEST,
-                preferred_element_type=jnp.float32)
-            tiles = lines.shape[0] // 8
+
+    @pl.when(first == stations - block)
+    def _():
+        lines = jnp.dot(
+            shapes[...], basis[...], precision=lax.Precision.HIGHEST,
+            preferred_element_type=jnp.float32)
+        tiles = m // 8
+        for p in range(planes):
             for h in range(2):
-                amp[pl.ds((2 * p + h) * tiles, tiles)] = (
-                    lines[:, h * LANES:(h + 1) * LANES].reshape(tiles, 8, LANES))
+                at = (2 * p + h) * tiles
+                amp[at:at + tiles] = (
+                    lines[p * m:(p + 1) * m, h * LANES:(h + 1) * LANES].reshape(tiles, 8, LANES))
 
 
 def stencil(flow, rows_in, cols_in, swirl, diff, plane_index, modes, mode_order):
     stations, rows, cols = flow.shape
     planes = plane_index.shape[0]
     m = modes.shape[0]
+    block = 4
     f32 = jnp.float32
     smem = pl.BlockSpec(memory_space=pltpu.SMEM)
-    plane = pl.BlockSpec((1, rows, cols), lambda z: (z, 0, 0))
+    some = pl.BlockSpec((block, rows, cols), lambda z: (z, 0, 0))
 
     def whole(shape):
         return pl.BlockSpec(shape, lambda z: (0,) * len(shape))
@@ -255,20 +264,21 @@
             jax.ShapeDtypeStruct(flow.shape, f32),
             jax.ShapeDtypeStruct((tiles, 8, LANES), f32),
         ),
-        grid=(stations,),
+        grid=(stations // block,),
         in_specs=[
-            smem, smem, plane, whole(rows_in.shape), whole(cols_in.shape), whole((1, rows)),
+            smem, smem, some, whole(rows_in.shape), whole(cols_in.shape), whole((1, rows)),
             whole(diff.shape), whole(modes.shape), whole((PERIOD, 2 * K)),
         ],
-        out_specs=(plane, whole((tiles, 8, LANES))),
+        out_specs=(some, whole((tiles, 8, LANES))),
         scratch_shapes=[
             pltpu.VMEM((rows, cols), f32),
             pltpu.VMEM((rows, cols), f32),
             pltpu.VMEM((rows, cols), f32),
             pltpu.VMEM((m, rows), f32),
-            pltpu.VMEM((rows, PERIOD), f32),
+            pltpu.VMEM((block, rows, PERIOD), f32),
+            pltpu.VMEM((planes * m, PERIOD), f32),
         ],
-        compiler_params=pltpu.CompilerParams(vmem_limit_bytes=32 * MIB),
+        compiler_params=pltpu.CompilerParams(vmem_limit_bytes=40 * MIB),
         name="stencil",
     )(plane_index, mode_order, flow, rows_in, cols_in, swirl.reshape(1, rows), diff, modes,
       jnp.asarray(dft_basis()))

time: 83.1 us -> 68.9 us (0.83); the launches traced: 82.1 us -> 68.9 us
  Pallas kernels: 80.5 us -> 67.3 us
    pallas_call x1, Pallas kernels: 44.9 us -> 31.7 us  [stencil(): pl.pallas_call(functools.partial(stencil_kernel, planes), out_shape=(jax....]
where the time goes in v2:
time: 68.9 us
  Pallas kernels  67.3 us (98%)
  local copies, waits for them, and re-layouts  0.82 us (1%)
  between operations  0.74 us (1%)
    pallas_call x1, Pallas kernels, stencil(): pl.pallas_call(functools.partial(stencil_kernel, planes), out_shape=(jax....  31.7 us
    pallas_call x1, Pallas kernels, amplitude_sum(): pl.pallas_call(functools.partial(sum_kernel, sizes), out_shape=jax.ShapeD...  21.6 us
    pallas_call x1, Pallas kernels, halo(): pl.pallas_call(functools.partial(halo_kernel, passages, spans, chunks), o...  14 us

profile of v2, /device:TPU:0, one launch (start us, length us, event | category | flops | bytes accessed | tf_op | source)
XLA Modules:
  0.0 68.9 jit_solution(12896652967526038858)
XLA Ops:
  0.6 0.0 copy-start.1
  0.6 0.0 copy-start.5
  0.7 0.0 copy-start.2
  0.7 0.0 copy-start.4
  0.7 0.0 copy-start
  0.7 0.0 copy-start.3
  0.7 14.0 %halo.1 = (f32[2,32,1024]{2,1,0:T(8,128)S(1)}, f32[2,64,128]{2,1,0:T(8,128)S(1)}) custom-call(f32[32,256,1024]{2,1,0:T(8,128)} %flow.3), custom_call_target="tpu_custom_call" | custom-call | tf_op jit(solution)/shard_map/halo/pallas_call | solution.py:146
  14.8 0.0 copy-done.1
  14.8 0.0 copy-done.5
  14.8 0.0 copy-done.2
  14.8 0.0 copy-done.4
  14.8 0.0 copy-done
  14.8 0.0 copy-done.3
  14.8 31.7 %stencil.1 = (f32[32,256,1024]{2,1,0:T(8,128)}, f32[128,8,128]{2,1,0:T(8,128)S(1)}) custom-call(s32[8]{0:T(128)S(1)} %copy-done.4, s32[64]{0:T(128)S(1)} %copy-done.5, f32[32,256,1024]{2,1,0:T(8,128)} %flow.3, f32[2,32,1024]{2,1,0:T(8,128)S(1)} %get-tuple-element.6.rows_in, f32[2,64,128]{2,1,0:T(8,128)S(1)} %get-tuple-element.7.cols_in, ...), custom_call_target="tpu_custom_call" | custom-call | tf_op jit(solution)/shard_map/stencil/pallas_call | solution.py:261
  46.6 21.6 %amplitude_sum.1 = f32[8,64,256]{2,1,0:T(8,128)S(1)} custom-call(f32[128,8,128]{2,1,0:T(8,128)S(1)} %get-tuple-element.9.amp), custom_call_target="tpu_custom_call" | custom-call | tf_op jit(solution)/shard_map/amplitude_sum/pallas_call | solution.py:371
  68.1 0.8 %copy.10 = f32[8,64,256]{2,1,0:T(8,128)} copy(f32[8,64,256]{2,1,0:T(8,128)S(1)} %amplitude_sum.1) | data formatting | bytes 1048576
Async XLA Ops:
  0.6 14.1 %copy-start.1 = (f32[256,256]{1,0:T(8,128)S(1)}, f32[256,256]{1,0:T(8,128)}, u32[]{:S(2)}) copy-start(f32[256,256]{1,0:T(8,128)} %constant.2.clone.basis) | copy-start | bytes 786436
  0.6 14.1 %copy-start.5 = (s32[64]{0:T(128)S(1)}, s32[64]{0:T(128)}, u32[]{:S(2)}) copy-start(s32[64]{0:T(128)} %mode_order.1) | copy-start | bytes 772
  0.7 14.1 %copy-start.2 = (f32[64,256]{1,0:T(8,128)S(1)}, f32[64,256]{1,0:T(8,128)}, u32[]{:S(2)}) copy-start(f32[64,256]{1,0:T(8,128)} %modes.1) | copy-start | bytes 196612
  0.7 14.1 %copy-start.4 = (s32[8]{0:T(128)S(1)}, s32[8]{0:T(128)}, u32[]{:S(2)}) copy-start(s32[8]{0:T(128)} %plane_index.1) | copy-start | bytes 100
  0.7 14.1 %copy-start = (f32[256,1024]{1,0:T(8,128)S(1)}, f32[256,1024]{1,0:T(8,128)}, u32[]{:S(2)}) copy-start(f32[256,1024]{1,0:T(8,128)} %diff.1) | copy-start | bytes 3145732
  0.7 14.1 %copy-start.3 = (f32[256]{0:T(256)S(1)}, f32[256]{0:T(256)}, u32[]{:S(2)}) copy-start(f32[256]{0:T(256)} %param.8) | copy-start | bytes 3076

commit v3 on v2

--- a/solution.py
+++ b/solution.py
@@ -105,9 +105,9 @@
 
     lane = lax.broadcasted_iota(jnp.int32, (per, LANES), 1)
 
-    def pack(z, carry):
+    def pack(i, carry):
         a, b = carry
-        for g in range(groups):
+        for z, g in [(4 * i + j, g) for j in range(4) for g in range(groups)]:
             spot = g * stations + z
             part = pl.ds(g * per, per)
             a = jnp.where(lane == spot, pltpu.roll(left[z, part, :], spot, 1), a)
@@ -119,7 +119,7 @@
     for c in range(chunks):
         for copy in loads(c):
             copy.wait()
-        carry = lax.fori_loop(c * step, (c + 1) * step, pack, carry)
+        carry = lax.fori_loop(c * step // 4, (c + 1) * step // 4, pack, carry)
     cols_send[0], cols_send[1] = carry
     to_west.start()
     to_east.start()
@@ -284,7 +284,7 @@
       jnp.asarray(dft_basis()))
 
 
-def sum_kernel(sizes, amp, out, acc, full, *rest):
+def sum_kernel(sizes, jobs, amp, out, acc, full, *rest):
     recvs, (send_sem, recv_sem, send_sem2, recv_sem2) = rest[:3], rest[3:]
     cores, xs, zs = sizes
     span = lax.axis_index("span")
@@ -307,52 +307,64 @@
             pl.semaphore_signal(barrier, inc=1, device_id=peer(s, k), device_id_type=MESH)
     pl.semaphore_wait(barrier, sum(sizes) - 3)
 
-    size = amp.shape[0]
-    base = 0
-    bases, widths = [], []
-    index = 0
-    firsts = []
-    for s in range(3):
-        width = size // sizes[s]
-        source = amp if s == 0 else acc
-        firsts.append(index)
-        copies = []
-        for d, k in others(s):
-            copy = pltpu.make_async_remote_copy(
-                src_ref=source.at[pl.ds(base + k * width, width)], dst_ref=recvs[s].at[d - 1],
-                send_sem=send_sem.at[index], recv_sem=recv_sem.at[index],
-                device_id=peer(s, k), device_id_type=MESH)
-            copy.start()
-            copies.append(copy)
-            index += 1
-        base = base + mine[s] * width
-        size = width
-        bases.append(base)
-        widths.append(width)
-        for copy in copies:
-            copy.wait()
-        part = pl.ds(base, width)
-        total = source[part]
-        for d in range(1, sizes[s]):
-            total = total + recvs[s][d - 1]
-        if s < 2:
-            acc[part] = total
-        else:
-            full[part] = total
-
-    for s in (2, 1, 0):
-        part = pl.ds(bases[s], widths[s])
-        copies = []
-        for d, k in others(s):
-            at = firsts[s] + d - 1
-            copy = pltpu.make_async_remote_copy(
-                src_ref=full.at[part], dst_ref=full.at[part],
-                send_sem=send_sem2.at[at], recv_sem=recv_sem2.at[at],
-                device_id=peer(s, k), device_id_type=MESH)
-            copy.start()
-            copies.append(copy)
-        for copy in copies:
-            copy.wait()
+    tiles = amp.shape[0] // jobs
+    each = sum(sizes) - 3
+
+    class Job:
+        def __init__(self, number):
+            self.order = (0, 1, 2) if number % 2 == 0 else (0, 2, 1)
+            self.number = number
+            self.base, self.size = number * tiles, tiles
+            self.parts = []
+            self.copies = []
+
+        def at(self, s, d):
+            return self.number * each + sum(sizes[:s]) - s + d - 1
+
+        def start(self, step):
+            gather = step >= 3
+            s = self.order[5 - step if gather else step]
+            width = self.size // sizes[s]
+            self.copies = []
+            for d, k in others(s):
+                n = self.at(s, d)
+                if gather:
+                    part = self.parts[5 - step]
+                    source, target = full.at[part], full.at[part]
+                    sems = (send_sem2.at[n], recv_sem2.at[n])
+                else:
+                    source = (amp if step == 0 else acc).at[pl.ds(self.base + k * width, width)]
+                    target = recvs[s].at[self.number, d - 1, pl.ds(0, width)]
+                    sems = (send_sem.at[n], recv_sem.at[n])
+                copy = pltpu.make_async_remote_copy(
+                    src_ref=source, dst_ref=target, send_sem=sems[0], recv_sem=sems[1],
+                    device_id=peer(s, k), device_id_type=MESH)
+                copy.start()
+                self.copies.append(copy)
+
+        def finish(self, step):
+            for copy in self.copies:
+                copy.wait()
+            if step >= 3:
+                return
+            s = self.order[step]
+            width = self.size // sizes[s]
+            self.base, self.size = self.base + mine[s] * width, width
+            part = pl.ds(self.base, width)
+            self.parts.append(part)
+            total = (amp if step == 0 else acc)[part]
+            for d in range(1, sizes[s]):
+                total = total + recvs[s][self.number, d - 1, :width]
+            (acc if step < 2 else full)[part] = total
+
+    work = [Job(number) for number in range(jobs)]
+    for job in work:
+        job.start(0)
+    for step in range(6):
+        for job in work:
+            job.finish(step)
+            if step < 5:
+                job.start(step + 1)
 
     planes, m, _ = out.shape
     tiles = m // 8
@@ -365,19 +377,21 @@
 def amplitude_sum(amp, planes, m, sizes):
     f32 = jnp.float32
     tiles = amp.shape[0]
-    widths = [tiles // math.prod(sizes[:s + 1]) for s in range(3)]
+    jobs = 4 if tiles % (4 * math.prod(sizes)) == 0 else 1
+    cores, xs, zs = sizes
+    widths = [tiles // jobs // n for n in (cores, cores * xs, cores * zs)]
     total = sum(sizes) - 3
     vmem = pl.BlockSpec(memory_space=pltpu.VMEM)
     return pl.pallas_call(
-        functools.partial(sum_kernel, sizes),
+        functools.partial(sum_kernel, sizes, jobs),
         out_shape=jax.ShapeDtypeStruct((planes, m, 2 * K), f32),
         in_specs=[vmem],
         out_specs=vmem,
         scratch_shapes=[
             pltpu.VMEM((tiles, 8, LANES), f32),
             pltpu.VMEM((tiles, 8, LANES), f32),
-            *[pltpu.VMEM((max(n - 1, 1), w, 8, LANES), f32) for n, w in zip(sizes, widths)],
-            *[pltpu.SemaphoreType.DMA((total,)) for _ in range(4)],
+            *[pltpu.VMEM((jobs, max(n - 1, 1), w, 8, LANES), f32) for n, w in zip(sizes, widths)],
+            *[pltpu.SemaphoreType.DMA((jobs * total,)) for _ in range(4)],
         ],
         compiler_params=pltpu.CompilerParams(
             collective_id=1, has_side_effects=True, vmem_limit_bytes=16 * MIB),

time: 68.9 us -> 65.8 us (0.955)
  Pallas kernels: 67.3 us -> 63.9 us
    pallas_call x1, Pallas kernels: 21.6 us -> 19.8 us  [amplitude_sum(): pl.pallas_call(functools.partial(sum_kernel, sizes, jobs), out_shape=jax....]
    pallas_call x1, Pallas kernels: 14 us -> 12.4 us  [halo(): pl.pallas_call(functools.partial(halo_kernel, passages, spans, chunks), o...]
where the time goes in v3:
time: 65.8 us; the launch traced here: 65.5 us
  Pallas kernels  63.9 us (97%)
  local copies, waits for them, and re-layouts  0.82 us (1%)
  between operations  0.74 us (1%)
    pallas_call x1, Pallas kernels, stencil(): pl.pallas_call(functools.partial(stencil_kernel, planes), out_shape=(jax....  31.7 us
    pallas_call x1, Pallas kernels, amplitude_sum(): pl.pallas_call(functools.partial(sum_kernel, sizes, jobs), out_shape=jax....  19.8 us
    pallas_call x1, Pallas kernels, halo(): pl.pallas_call(functools.partial(halo_kernel, passages, spans, chunks), o...  12.4 us

profile of v3, /device:TPU:0, one launch (start us, length us, event | category | flops | bytes accessed | tf_op | source)
XLA Modules:
  0.0 65.5 jit_solution(14670224016752190734)
XLA Ops:
  0.6 0.0 copy-start.1
  0.6 0.0 copy-start.5
  0.7 0.0 copy-start.2
  0.7 0.0 copy-start.4
  0.7 0.0 copy-start
  0.7 0.0 copy-start.3
  0.7 12.4 %halo.1 = (f32[2,32,1024]{2,1,0:T(8,128)S(1)}, f32[2,64,128]{2,1,0:T(8,128)S(1)}) custom-call(f32[32,256,1024]{2,1,0:T(8,128)} %flow.3), custom_call_target="tpu_custom_call" | custom-call | tf_op jit(solution)/shard_map/halo/pallas_call | solution.py:146
  13.1 0.0 copy-done.1
  13.2 0.0 copy-done.5
  13.2 0.0 copy-done.2
  13.2 0.0 copy-done.4
  13.2 0.0 copy-done
  13.2 0.0 copy-done.3
  13.2 31.7 %stencil.1 = (f32[32,256,1024]{2,1,0:T(8,128)}, f32[128,8,128]{2,1,0:T(8,128)S(1)}) custom-call(s32[8]{0:T(128)S(1)} %copy-done.4, s32[64]{0:T(128)S(1)} %copy-done.5, f32[32,256,1024]{2,1,0:T(8,128)} %flow.3, f32[2,32,1024]{2,1,0:T(8,128)S(1)} %get-tuple-element.6.rows_in, f32[2,64,128]{2,1,0:T(8,128)S(1)} %get-tuple-element.7.cols_in, ...), custom_call_target="tpu_custom_call" | custom-call | tf_op jit(solution)/shard_map/stencil/pallas_call | solution.py:261
  44.9 19.8 %amplitude_sum.1 = f32[8,64,256]{2,1,0:T(8,128)S(1)} custom-call(f32[128,8,128]{2,1,0:T(8,128)S(1)} %get-tuple-element.9.amp), custom_call_target="tpu_custom_call" | custom-call | tf_op jit(solution)/shard_map/amplitude_sum/pallas_call | solution.py:385
  64.7 0.8 %copy.10 = f32[8,64,256]{2,1,0:T(8,128)} copy(f32[8,64,256]{2,1,0:T(8,128)S(1)} %amplitude_sum.1) | data formatting | bytes 1048576
Async XLA Ops:
  0.6 12.5 %copy-start.1 = (f32[256,256]{1,0:T(8,128)S(1)}, f32[256,256]{1,0:T(8,128)}, u32[]{:S(2)}) copy-start(f32[256,256]{1,0:T(8,128)} %constant.2.clone.basis) | copy-start | bytes 786436
  0.6 12.5 %copy-start.5 = (s32[64]{0:T(128)S(1)}, s32[64]{0:T(128)}, u32[]{:S(2)}) copy-start(s32[64]{0:T(128)} %mode_order.1) | copy-start | bytes 772
  0.7 12.5 %copy-start.2 = (f32[64,256]{1,0:T(8,128)S(1)}, f32[64,256]{1,0:T(8,128)}, u32[]{:S(2)}) copy-start(f32[64,256]{1,0:T(8,128)} %modes.1) | copy-start | bytes 196612
  0.7 12.5 %copy-start.4 = (s32[8]{0:T(128)S(1)}, s32[8]{0:T(128)}, u32[]{:S(2)}) copy-start(s32[8]{0:T(128)} %plane_index.1) | copy-start | bytes 100
  0.7 12.5 %copy-start = (f32[256,1024]{1,0:T(8,128)S(1)}, f32[256,1024]{1,0:T(8,128)}, u32[]{:S(2)}) copy-start(f32[256,1024]{1,0:T(8,128)} %diff.1) | copy-start | bytes 3145732
  0.7 12.5 %copy-start.3 = (f32[256]{0:T(256)S(1)}, f32[256]{0:T(256)}, u32[]{:S(2)}) copy-start(f32[256]{0:T(256)} %param.8) | copy-start | bytes 3076

commit v4 on v3

--- a/solution.py
+++ b/solution.py
@@ -107,7 +107,7 @@
 
     def pack(i, carry):
         a, b = carry
-        for z, g in [(4 * i + j, g) for j in range(4) for g in range(groups)]:
+        for z, g in [(step * i + j, g) for j in range(step) for g in range(groups)]:
             spot = g * stations + z
             part = pl.ds(g * per, per)
             a = jnp.where(lane == spot, pltpu.roll(left[z, part, :], spot, 1), a)
@@ -119,7 +119,7 @@
     for c in range(chunks):
         for copy in loads(c):
             copy.wait()
-        carry = lax.fori_loop(c * step // 4, (c + 1) * step // 4, pack, carry)
+        carry = pack(c, carry)
     cols_send[0], cols_send[1] = carry
     to_west.start()
     to_east.start()

time: 65.8 us -> 65.4 us (level)
  no operation moved by 1% of the time
where the time goes in v4:
time: 65.4 us; the launch traced here: 65.3 us
  Pallas kernels  63.7 us (97%)
  local copies, waits for them, and re-layouts  0.82 us (1%)
  between operations  0.74 us (1%)
    pallas_call x1, Pallas kernels, stencil(): pl.pallas_call(functools.partial(stencil_kernel, planes), out_shape=(jax....  31.6 us
    pallas_call x1, Pallas kernels, amplitude_sum(): pl.pallas_call(functools.partial(sum_kernel, sizes, jobs), out_shape=jax....  19.8 us
    pallas_call x1, Pallas kernels, halo(): pl.pallas_call(functools.partial(halo_kernel, passages, spans, chunks), o...  12.3 us

profile of v4, /device:TPU:0, one launch (start us, length us, event | category | flops | bytes accessed | tf_op | source)
XLA Modules:
  0.0 65.3 jit_solution(9435729857023899075)
XLA Ops:
  0.6 0.0 copy-start.1
  0.6 0.0 copy-start.5
  0.7 0.0 copy-start.2
  0.7 0.0 copy-start.4
  0.7 0.0 copy-start
  0.7 0.0 copy-start.3
  0.7 12.3 %halo.1 = (f32[2,32,1024]{2,1,0:T(8,128)S(1)}, f32[2,64,128]{2,1,0:T(8,128)S(1)}) custom-call(f32[32,256,1024]{2,1,0:T(8,128)} %flow.3), custom_call_target="tpu_custom_call" | custom-call | tf_op jit(solution)/shard_map/halo/pallas_call | solution.py:146
  13.0 0.0 copy-done.1
  13.0 0.0 copy-done.5
  13.0 0.0 copy-done.2
  13.0 0.0 copy-done.4
  13.0 0.0 copy-done
  13.0 0.0 copy-done.3
  13.0 31.6 %stencil.1 = (f32[32,256,1024]{2,1,0:T(8,128)}, f32[128,8,128]{2,1,0:T(8,128)S(1)}) custom-call(s32[8]{0:T(128)S(1)} %copy-done.4, s32[64]{0:T(128)S(1)} %copy-done.5, f32[32,256,1024]{2,1,0:T(8,128)} %flow.3, f32[2,32,1024]{2,1,0:T(8,128)S(1)} %get-tuple-element.6.rows_in, f32[2,64,128]{2,1,0:T(8,128)S(1)} %get-tuple-element.7.cols_in, ...), custom_call_target="tpu_custom_call" | custom-call | tf_op jit(solution)/shard_map/stencil/pallas_call | solution.py:261
  44.6 19.8 %amplitude_sum.1 = f32[8,64,256]{2,1,0:T(8,128)S(1)} custom-call(f32[128,8,128]{2,1,0:T(8,128)S(1)} %get-tuple-element.9.amp), custom_call_target="tpu_custom_call" | custom-call | tf_op jit(solution)/shard_map/amplitude_sum/pallas_call | solution.py:385
  64.5 0.8 %copy.10 = f32[8,64,256]{2,1,0:T(8,128)} copy(f32[8,64,256]{2,1,0:T(8,128)S(1)} %amplitude_sum.1) | data formatting | bytes 1048576
Async XLA Ops:
  0.6 12.3 %copy-start.1 = (f32[256,256]{1,0:T(8,128)S(1)}, f32[256,256]{1,0:T(8,128)}, u32[]{:S(2)}) copy-start(f32[256,256]{1,0:T(8,128)} %constant.2.clone.basis) | copy-start | bytes 786436
  0.6 12.3 %copy-start.5 = (s32[64]{0:T(128)S(1)}, s32[64]{0:T(128)}, u32[]{:S(2)}) copy-start(s32[64]{0:T(128)} %mode_order.1) | copy-start | bytes 772
  0.7 12.3 %copy-start.2 = (f32[64,256]{1,0:T(8,128)S(1)}, f32[64,256]{1,0:T(8,128)}, u32[]{:S(2)}) copy-start(f32[64,256]{1,0:T(8,128)} %modes.1) | copy-start | bytes 196612
  0.7 12.3 %copy-start.4 = (s32[8]{0:T(128)S(1)}, s32[8]{0:T(128)}, u32[]{:S(2)}) copy-start(s32[8]{0:T(128)} %plane_index.1) | copy-start | bytes 100
  0.7 12.3 %copy-start = (f32[256,1024]{1,0:T(8,128)S(1)}, f32[256,1024]{1,0:T(8,128)}, u32[]{:S(2)}) copy-start(f32[256,1024]{1,0:T(8,128)} %diff.1) | copy-start | bytes 3145732
  0.7 12.3 %copy-start.3 = (f32[256]{0:T(256)S(1)}, f32[256]{0:T(256)}, u32[]{:S(2)}) copy-start(f32[256]{0:T(256)} %param.8) | copy-start | bytes 3076
